TPU v7x, 1024 devices: a whole 4x4x32 slice. The times are simulated.
1024 devices in a mesh: fsdp: 64 (over z, x_hi), tp: 8 (over y, x_lo), rep: 2 (over core).
Axes of the slice: x: 4 (x_hi: 2, x_lo: 2; x = x_hi * 2 + x_lo), y: 4, z: 32, core: 2. Of those that a mesh axis runs over, the one named last changes fastest.
Arguments:
- base_weight: bfloat16 [64, 1024, 7168], P('fsdp', 'tp'), may hold values from -0.125 to 0.125
- delta_codes: bfloat16 [64, 1024, 7168], P(None, ('tp', 'rep'), 'fsdp'), may hold values from -448 to 448
- block_scales: float32 [64, 8, 56], P('fsdp', 'tp'), may hold values from 2e-05 to 0.0001
- hidden_acts: bfloat16 [2, 512, 8, 2, 1024], P(None, ('fsdp', 'rep'), None, None, 'tp'), may hold values from -6 to 6
- expert_ids: int32 [2, 512, 8], P(None, ('fsdp', 'rep')), may hold values from 0 to 31, all different within a row; in each aligned block of 4 rows (0 to 3, 4 to 7, ..., all dimensions but the last counted through in order) at most 2 rows name the same one
- gate_weights: float32 [2, 512, 8], P(None, ('fsdp', 'rep')), may hold values from 0.1 to 1
Outputs:
- mixed_rows: bfloat16 [2, 512, 7168], P(None, ('fsdp', 'rep'), 'tp')
Inputs may be any that keep to these rules, and one draw needn't show every extreme that they name: `expert_ids`: within the 4 rows of one device in one step (aligned blocks), no expert is named by more than 2 rows, a bound that some block reaches; a row names 8 different experts.
All inputs are finite; a program needn't handle non-finite values.
Results may differ from a plain program's by a relative error of at most 0.015.
Values may be sent and summed in bfloat16 or wider, within the bound.
A program may use at most 64 MiB of HBM per device.

v0:
```python
import jax
import jax.numpy as jnp
from jax import lax
from jax.sharding import PartitionSpec as P


def dequantize(base_rows, code_rows, scale_blocks):
    held_pairs, row_span, model_width = code_rows.shape
    block_rows = base_rows.shape[1] // scale_blocks.shape[1]
    blocks_wide = scale_blocks.shape[2]
    row_scales = jnp.repeat(scale_blocks, block_rows, axis=1)
    scaled = (
        code_rows.astype(jnp.float32).reshape(
            held_pairs, row_span, blocks_wide, model_width // blocks_wide
        )
        * row_scales[..., None]
    )
    return (
        base_rows.astype(jnp.float32) + scaled.reshape(held_pairs, row_span, model_width)
    ).astype(jnp.bfloat16)


def shards(base_weight, delta_codes, block_scales, hidden_acts, expert_ids, gate_weights):
    held_pairs, unit_count, model_width = base_weight.shape
    arrived = lax.all_to_all(delta_codes, "fsdp", split_axis=0, concat_axis=2, tiled=True)
    codes_all = lax.all_gather(arrived, "rep", axis=1, tiled=True)
    weights = dequantize(base_weight, codes_all, block_scales)
    owners = lax.axis_size("fsdp")
    experts = owners * held_pairs // 2
    step_count, row_count, top_count = expert_ids.shape
    capacity = min(row_count, max(2, 2 * row_count * top_count // experts))
    slot_count = row_count * top_count
    slot_index = jnp.arange(slot_count, dtype=jnp.int32)
    expert_range = jnp.arange(experts, dtype=jnp.int32)
    cap_range = jnp.arange(capacity, dtype=jnp.int32)
    results = []
    for step_index in range(step_count):
        flat_ids = expert_ids[step_index].reshape(slot_count)
        flat_gates = gate_weights[step_index].reshape(slot_count)
        same_expert = flat_ids[:, None] == flat_ids[None, :]
        before = slot_index[None, :] < slot_index[:, None]
        position = jnp.sum(jnp.where(same_expert & before, 1, 0), axis=1).astype(jnp.int32)
        select = (flat_ids[None, None, :] == expert_range[:, None, None]) & (
            position[None, None, :] == cap_range[None, :, None]
        )
        activations = hidden_acts[step_index].reshape(slot_count, 2, unit_count)
        packed = jnp.einsum(
            "ecs,sph->epch",
            select.astype(jnp.bfloat16),
            activations,
            preferred_element_type=jnp.float32,
        ).astype(jnp.bfloat16)
        packed = packed.reshape(owners, held_pairs, capacity, unit_count)
        received = lax.all_to_all(packed, "fsdp", split_axis=0, concat_axis=0, tiled=True)
        combine = (
            (select.astype(jnp.float32) * flat_gates[None, None, :])
            .reshape(experts, capacity, row_count, top_count)
            .sum(axis=3)
        )
        partial_value = jnp.einsum(
            "sgch,ghd->sgcd", received, weights, preferred_element_type=jnp.float32
        ).astype(jnp.bfloat16)
        totals = lax.psum_scatter(
            partial_value.astype(jnp.float32).astype(jnp.bfloat16),
            "tp",
            scatter_dimension=3,
            tiled=True,
        ).astype(jnp.float32)
        returned = lax.all_to_all(
            totals.astype(jnp.bfloat16), "fsdp", split_axis=0, concat_axis=0, tiled=True
        ).astype(totals.dtype)
        paired = returned.reshape(experts, 2, capacity, returned.shape[3]).sum(axis=1)
        mixed_rows = jnp.einsum("ecr,ecd->rd", combine, paired, precision=lax.Precision.HIGHEST)
        results.append(mixed_rows.astype(jnp.bfloat16))
    return jnp.stack(results)


def solution(mesh):
    placed = (
        P("fsdp", "tp", None),
        P(None, ("tp", "rep"), "fsdp"),
        P("fsdp", "tp", None),
        P(None, ("fsdp", "rep"), None, None, "tp"),
        P(None, ("fsdp", "rep"), None),
        P(None, ("fsdp", "rep"), None),
    )
    return jax.shard_map(
        shards,
        mesh=mesh,
        in_specs=placed,
        out_specs=P(None, ("fsdp", "rep"), "tp"),
        check_vma=False,
    )
```

profile of v0, /device:TPU:24, one launch (start us, length us, event | category | flops | bytes accessed | tf_op | source)
XLA Modules:
  0.0 395.7 jit_solution(11302761286010477915)
XLA Ops:
  6.5 141.8 %all_to_all.38 = bf16[64,64,112]{2,1,0:T(8,128)(2,1)S(1)} all-to-all(bf16[64,64,112]{2,1,0:T(8,128)(2,1)} %param.7), channel_id=1, replica_groups=mesh['fsdp'=64,'tp'=8,'rep'=2] {'fsdp'}, dimensions={0} | all-to-all | bytes 1835008 | tf_op jit(solution)/shard_map/all_to_all | solution.py:25
  148.3 0.7 copy.38
  149.0 0.0 copy-start.3
  149.0 0.0 copy-start.2
  149.0 0.0 copy-start.1
  149.0 3.2 all_to_all.28
  152.3 0.0 all-gather.2.cloned.1.call-update
  152.3 0.1 eq.138
  152.4 0.2 select_reduce_fusion.3
  152.7 0.1 fusion.3
  152.8 0.6 copy.41
  153.5 5.3 %all-to-all-start.1 = ((bf16[64,1,2,128]{3,2,1,0:T(2,128)(2,1)}), bf16[64,1,2,128]{3,2,1,0:T(2,128)(2,1)S(1)}, u32[]{:S(2)}, u32[]{:S(2)}) async-start(bf16[64,1,2,128]{3,2,1,0:T(2,128)(2,1)} %copy.41), calls=%async_computation.1 | async-start | bytes 65536 | tf_op jit(solution)/shard_map/all_to_all | solution.py:54
  158.8 0.0 reduce-scatter.7.cloned.1.call-start
  158.9 0.1 broadcast_bitcast_fusion
  159.0 25.0 %all-to-all-done.1 = bf16[64,1,2,128]{3,2,1,0:T(2,128)(2,1)S(1)} async-done(((bf16[64,1,2,128]{3,2,1,0:T(2,128)(2,1)}), bf16[64,1,2,128]{3,2,1,0:T(2,128)(2,1)S(1)}, u32[]{:S(2)}, u32[]{:S(2)}) %all-to-all-start.1) | async-done | bytes 32800 | tf_op jit(solution)/shard_map/all_to_all | solution.py:54
  183.9 3.7 fusion
  187.6 8.6 %copy.53 = bf16[64,1,2,7168]{0,2,1,3:T(2,128)(2,1)} copy(bf16[64,1,2,7168]{3,0,2,1:T(8,128)(2,1)} %fusion) | data formatting | bytes 3670016
  196.2 7.0 %reshape.201 = bf16[7168,128]{1,0:T(8,128)(2,1)} reshape(bf16[7168,1,2,64]{3,2,1,0:T(2,128)(2,1)} %bitcast.94) | data formatting | bytes 3670016
  203.2 0.0 reduce-scatter.7.cloned.1.call-update
  203.2 0.0 reduce-scatter.9.cloned.1.call-start
  203.3 0.1 eq.155
  203.4 0.2 select_reduce_fusion.2
  203.6 0.1 fusion.4
  203.8 31.3 %all_to_all.39 = bf16[64,1,2,128]{3,2,1,0:T(2,128)(2,1)S(1)} all-to-all(bf16[64,1,2,128]{3,2,1,0:T(2,128)(2,1)S(1)} %copy.47), channel_id=1, replica_groups=mesh['fsdp'=64,'tp'=8,'rep'=2] {'fsdp'}, dimensions={0} | all-to-all | bytes 65536 | tf_op jit(solution)/shard_map/all_to_all | solution.py:54
  235.1 3.7 fusion.1
  238.8 8.6 %copy.55 = bf16[64,1,2,7168]{0,2,1,3:T(2,128)(2,1)} copy(bf16[64,1,2,7168]{3,0,2,1:T(8,128)(2,1)} %fusion.1) | data formatting | bytes 3670016
  247.4 7.0 %reshape.203 = bf16[7168,128]{1,0:T(8,128)(2,1)} reshape(bf16[7168,1,2,64]{3,2,1,0:T(2,128)(2,1)} %bitcast.95) | data formatting | bytes 3670016
  254.4 0.0 reduce-scatter.9.cloned.1.call-update
  254.5 0.0 copy-start.4
  254.5 0.0 reduce-scatter.7.cloned.1.call-done
  254.5 1.2 reshape.202
  255.7 1.4 copy.43
  257.0 19.9 %all-to-all-start.2 = ((bf16[64,1,2,896]{3,2,1,0:T(2,128)(2,1)}), bf16[64,1,2,896]{3,2,1,0:T(2,128)(2,1)S(1)}, u32[]{:S(2)}, u32[]{:S(2)}) async-start(bf16[64,1,2,896]{3,2,1,0:T(2,128)(2,1)} %copy.43), calls=%async_computation.2 | async-start | bytes 458752 | tf_op jit(solution)/shard_map/all_to_all | solution.py:69
  276.9 42.3 %reduce-scatter.9.cloned.1.call-done = bf16[896,128]{1,0:T(8,128)(2,1)} async-done(((bf16[7168,128]{1,0:T(8,128)(2,1)}), bf16[896,128]{1,0:T(8,128)(2,1)}) %reduce-scatter.9.cloned.1.call-update) | async-done | bytes 229392
  319.3 1.2 reshape.204
  320.4 1.4 copy.49
  321.8 25.3 %all-to-all-start.4 = ((bf16[64,1,2,896]{3,2,1,0:T(2,128)(2,1)}), bf16[64,1,2,896]{3,2,1,0:T(2,128)(2,1)S(1)}, u32[]{:S(2)}, u32[]{:S(2)}) async-start(bf16[64,1,2,896]{3,2,1,0:T(2,128)(2,1)} %copy.49), calls=%async_computation.4 | async-start | bytes 458752 | tf_op jit(solution)/shard_map/all_to_all | solution.py:69
  347.1 0.1 eq.159
  347.2 0.1 eq.142
  347.3 0.1 iota_compare_fusion.4
  347.4 0.1 iota_compare_fusion.1
  347.5 0.1 select_reduce_fusion
  347.6 0.3 convert_reduce_fusion.1
  347.9 39.8 %all-to-all-done.4 = bf16[64,1,2,896]{3,2,1,0:T(2,128)(2,1)S(1)} async-done(((bf16[64,1,2,896]{3,2,1,0:T(2,128)(2,1)}), bf16[64,1,2,896]{3,2,1,0:T(2,128)(2,1)S(1)}, u32[]{:S(2)}, u32[]{:S(2)}) %all-to-all-start.4) | async-done | bytes 229408 | tf_op jit(solution)/shard_map/all_to_all | solution.py:69
  387.7 0.3 convert_reduce_fusion
  388.0 0.3 fusion.8
  388.3 0.3 fusion.7
  388.6 0.6 pad_maximum_fusion
  (21 shorter events, 0.2 us)
Async XLA Ops:
  6.5 152.3 %copy-start = (f32[1,1,56]{2,1,0:T(1,128)S(1)}, f32[1,1,56]{2,1,0:T(1,128)}, u32[]{:S(2)}) copy-start(f32[1,1,56]{2,1,0:T(1,128)} %param.8) | copy-start | bytes 676
  6.5 177.4 %all-gather.2.cloned.1.call-start = ((), (), s32[]{:S(2)}) async-start(), calls=%async_computation.7 | async-start | bytes 2752512 | tf_op jit(solution)/shard_map/all_gather | solution.py:26
  149.0 3.3 copy-start.3
  149.0 3.6 copy-start.2
  149.0 34.9 %copy-start.1 = (bf16[1,128,7168]{2,1,0:T(8,128)(2,1)S(1)}, bf16[1,128,7168]{2,1,0:T(8,128)(2,1)}, u32[]{:S(2)}) copy-start(bf16[1,128,7168]{2,1,0:T(8,128)(2,1)} %param.6) | copy-start | bytes 5505028
  153.5 30.4 %all-to-all-start.1 = ((bf16[64,1,2,128]{3,2,1,0:T(2,128)(2,1)}), bf16[64,1,2,128]{3,2,1,0:T(2,128)(2,1)S(1)}, u32[]{:S(2)}, u32[]{:S(2)}) async-start(bf16[64,1,2,128]{3,2,1,0:T(2,128)(2,1)} %copy.41), calls=%async_computation.1 | async-start | bytes 65536 | tf_op jit(solution)/shard_map/all_to_all | solution.py:54
  158.8 95.7 %reduce-scatter.7.cloned.1.call-start = ((), (), s32[]{:S(2)}) async-start(), calls=%async_computation.8 | async-start | bytes 2064384
  203.2 116.0 %reduce-scatter.9.cloned.1.call-start = ((), (), s32[]{:S(2)}) async-start(), calls=%async_computation.9 | async-start | bytes 2064384
  254.5 92.9 %copy-start.4 = (f32[2,4,8]{2,1,0:T(4,128)S(1)}, f32[2,4,8]{2,1,0:T(4,128)}, u32[]{:S(2)}) copy-start(f32[2,4,8]{2,1,0:T(4,128)} %param.11) | copy-start | bytes 772
  257.0 64.8 %all-to-all-start.2 = ((bf16[64,1,2,896]{3,2,1,0:T(2,128)(2,1)}), bf16[64,1,2,896]{3,2,1,0:T(2,128)(2,1)S(1)}, u32[]{:S(2)}, u32[]{:S(2)}) async-start(bf16[64,1,2,896]{3,2,1,0:T(2,128)(2,1)} %copy.43), calls=%async_computation.2 | async-start | bytes 458752 | tf_op jit(solution)/shard_map/all_to_all | solution.py:69
  321.8 65.9 %all-to-all-start.4 = ((bf16[64,1,2,896]{3,2,1,0:T(2,128)(2,1)}), bf16[64,1,2,896]{3,2,1,0:T(2,128)(2,1)S(1)}, u32[]{:S(2)}, u32[]{:S(2)}) async-start(bf16[64,1,2,896]{3,2,1,0:T(2,128)(2,1)} %copy.49), calls=%async_computation.4 | async-start | bytes 458752 | tf_op jit(solution)/shard_map/all_to_all | solution.py:69
Sparse Core Ops, SparseCore 0:
  152.4 11.6 all-gather.1
  203.4 45.6 reduce-scatter.6
  254.6 64.6 reduce-scatter.8
where the time goes:
time: 398 us; the launch traced here: 396 us
  blocking collectives  173 us (43%)
  waiting for transfers between devices  107 us (27%)
  starting transfers between devices  50.7 us (13%)
  local copies, waits for them, and re-layouts  41.4 us (10%)
  between operations  13.3 us (3%)
  matrix products  8.22 us (2%)
    all_to_all x1, blocking collectives, shards(): lax.all_to_all(delta_codes, 'fsdp', split_axis=0, concat_axis=2, tiled=True)  142 us
    all_to_all x2, starting transfers between devices, shards(): lax.all_to_all(totals.astype(jnp.bfloat16), 'fsdp', split_axis=0, concat_...  45.2 us
    unnamed x5, waiting for transfers between devices  42.4 us
    all_to_all x2, waiting for transfers between devices, shards(): lax.all_to_all(totals.astype(jnp.bfloat16), 'fsdp', split_axis=0, concat_...  39.8 us
    unnamed x16, local copies, waits for them, and re-layouts  33.6 us
    all_to_all x1, blocking collectives, shards(): lax.all_to_all(packed, 'fsdp', split_axis=0, concat_axis=0, tiled=True)  31.3 us
    all_to_all x1, waiting for transfers between devices, shards(): lax.all_to_all(packed, 'fsdp', split_axis=0, concat_axis=0, tiled=True)  25 us
  transfers between devices with their start and end apart: 6, of which 3 were waited for; matrix products, arithmetic and copies ran while one was open for 7% of the time, Pallas kernels for 0%

commit v1 on v0

v1 whole, which is shorter than its diff:
```python
import jax
import jax.numpy as jnp
from jax import lax
from jax.experimental import pallas as pl
from jax.experimental.pallas import tpu as pltpu
from jax.sharding import PartitionSpec as P

MESH = pl.DeviceIdType.MESH
BF16 = jnp.bfloat16
F32 = jnp.float32


def position():
    f, t, r = lax.axis_index("fsdp"), lax.axis_index("tp"), lax.axis_index("rep")
    return f // 2, f % 2, t, r


def push(src, dst, send_sem, recv_sem, z, xh, t, r):
    return pltpu.make_async_remote_copy(
        src_ref=src,
        dst_ref=dst,
        send_sem=send_sem,
        recv_sem=recv_sem,
        device_id=(z * 2 + xh, t, r),
        device_id_type=MESH,
    )


def loop(low, high, body):
    def step(i, carry):
        body(i)
        return carry

    lax.fori_loop(low, high, step, jnp.int32(0))


def spread_kernel(
    planes, groups, disp, quarters, base, codes,
    slots, ring, weights, swapped,
    quad, local_sem, quad_send, quad_recv, disp_send, disp_recv, tp_send, tp_recv,
    w_send, w_recv, pair_send, pair_recv, code_send, code_recv,
    right_send, right_recv, left_send, left_recv,
):
    z, xh, t, r = position()
    home = xh * 2 + r
    place = xh * groups + t
    half_units = base.shape[0] // 2
    width = weights.shape[2]

    def hello(to_z, to_xh, to_t, to_r):
        pl.semaphore_signal(
            pltpu.get_barrier_semaphore(),
            inc=1,
            device_id=(to_z * 2 + to_xh, to_t, to_r),
            device_id_type=MESH,
        )

    loop(1, planes, lambda d: hello((z + d) % planes, xh, t, r))
    def hello_plane(j):
        other = (place + j) % (2 * groups)
        hello(z, other // groups, other % groups, r)
    loop(1, 2 * groups, hello_plane)
    hello(z, xh, t, 1 - r)
    hello(z, 1 - xh, t, 1 - r)

    def quad_copy(i):
        to = (home + i) % 4
        return push(quarters.at[to], quad.at[home], quad_send.at[i], quad_recv.at[i], z, to // 2, t, to % 2)

    def disp_copy(d):
        to = (z + d) % planes
        return push(disp.at[to], slots.at[t, z], disp_send.at[d], disp_recv.at[d], to, xh, t, r)

    def tp_copy(j):
        return push(slots.at[t], slots.at[t], tp_send.at[j], tp_recv.at[j], z, xh, (t + j) % groups, r)

    rows_here = pl.ds(pl.multiple_of(r * half_units, half_units), half_units)

    def w_columns(to_t):
        return pl.ds(pl.multiple_of(to_t * width, width), width)

    def w_copy(j):
        to = (place + j) % (2 * groups)
        return push(
            base.at[rows_here, w_columns(to % groups)],
            weights.at[t * 2 + xh, rows_here, :],
            w_send.at[j], w_recv.at[j], z, to // groups, to % groups, r,
        )

    def pair_copy():
        return push(weights.at[:, rows_here, :], weights.at[:, rows_here, :], pair_send, pair_recv, z, xh, t, 1 - r)

    def code_copy():
        return push(codes.at[:, 1 - xh], swapped.at[xh], code_send, code_recv, z, 1 - xh, t, r)

    def right_copy(i):
        block = ring.at[(z - i + planes) % planes]
        return push(block, block, right_send.at[i], right_recv.at[i], (z + 1) % planes, xh, t, r)

    def left_copy(i):
        block = ring.at[(z + i) % planes]
        return push(block, block, left_send.at[i], left_recv.at[i], (z + planes - 1) % planes, xh, t, r)

    own_disp = pltpu.make_async_copy(disp.at[z], slots.at[t, z], local_sem.at[0])
    own_w = pltpu.make_async_copy(
        base.at[rows_here, w_columns(t)], weights.at[t * 2 + xh, rows_here, :], local_sem.at[1]
    )
    own_codes = pltpu.make_async_copy(codes.at[:, xh], swapped.at[xh], local_sem.at[2])
    own_quad = pltpu.make_async_copy(quarters.at[home], quad.at[home], local_sem.at[3])
    own_disp.start()
    own_w.start()
    own_codes.start()
    own_quad.start()
    pl.semaphore_wait(pltpu.get_barrier_semaphore(), (planes - 1) + (2 * groups - 1) + 2)

    for i in range(1, 4):
        quad_copy(i).start()
    loop(1, planes, lambda d: disp_copy(d).start())
    own_quad.wait()
    for i in range(1, 4):
        quad_copy(i).wait()
    part = quarters.shape[1] - 16
    for i in range(4):
        ring[z, i * part:(i + 1) * part, :] = quad[i, :part, :]
    ring[z, 4 * part:, :] = (
        quad[0, part:, :] + quad[1, part:, :] + quad[2, part:, :] + quad[3, part:, :]
    )
    right_copy(0).start()
    left_copy(0).start()
    loop(1, 2 * groups, lambda j: w_copy(j).start())
    code_copy().start()

    right_steps = planes // 2
    left_steps = planes - 1 - right_steps

    def ring_step(i):
        right_copy(i - 1).wait_recv()
        right_copy(i).start()
        left_copy(i - 1).wait_recv()
        left_copy(i).start()

    middle = left_steps // 2
    loop(1, middle, ring_step)
    own_disp.wait()
    loop(1, planes, lambda d: disp_copy(d).wait())
    loop(1, groups, lambda j: tp_copy(j).start())
    loop(middle, left_steps, ring_step)
    own_w.wait()
    loop(1, 2 * groups, lambda j: w_copy(j).wait())
    pair_copy().start()
    right_copy(left_steps - 1).wait_recv()
    right_copy(left_steps).start()
    left_copy(left_steps - 1).wait_recv()
    right_copy(left_steps).wait_recv()
    loop(0, right_steps, lambda i: right_copy(i).wait_send())
    loop(0, left_steps, lambda i: left_copy(i).wait_send())
    loop(1, groups, lambda j: tp_copy(j).wait())
    own_codes.wait()
    code_copy().wait()
    pair_copy().wait()


def code_kernel(per, ring_ref, weight_ref, out_ref, wide):
    block = ring_ref[...]
    rows = per * 64
    lanes = 128
    tags = block[:, 128:, :].reshape(per * 16, lanes)
    lane_in = lax.broadcasted_iota(jnp.int32, (lanes, 4 * lanes), 0)
    lane_out = lax.broadcasted_iota(jnp.int32, (lanes, 4 * lanes), 1)
    named = []
    for home in range(4):
        pick = jnp.where(lane_in == home * 32 + (lane_out // lanes) * 8, 1.0, 0.0).astype(BF16)
        spread = jnp.dot(tags, pick, preferred_element_type=F32)
        named.append(spread.reshape(per, 1, 16, 4 * lanes))
    named = jnp.concatenate(named, axis=1).reshape(rows, 4 * lanes)
    upper = jnp.where(lax.broadcasted_iota(jnp.int32, (rows, 4 * lanes), 1) % lanes >= 64, 1.0, 0.0)
    named = (named - upper).astype(BF16)
    lane_in = lax.broadcasted_iota(jnp.int32, (lanes, 2 * lanes), 0)
    lane_out = lax.broadcasted_iota(jnp.int32, (lanes, 2 * lanes), 1)
    double = jnp.where(lane_in == (lane_out // lanes) * 64 + lane_out % 64, 1.0, 0.0).astype(BF16)
    acts = block[:, :128, :].reshape(per, 4, 2, 16, lanes)
    values, names = [], []
    for m in range(2):
        both = jnp.dot(
            acts[:, :, m].reshape(rows, lanes), double, preferred_element_type=F32
        ).astype(BF16)
        for j in range(2):
            values.append(both[:, j * lanes:(j + 1) * lanes])
            names.append(named[:, (m * 2 + j) * lanes:(m * 2 + j + 1) * lanes])
    pairs = weight_ref.shape[0] // lanes
    for pair in range(pairs):
        chosen = jnp.zeros((rows, lanes), BF16)
        for value, name in zip(values, names):
            chosen = jnp.where(name == jnp.asarray(2.0 * pair, BF16), value, chosen)
        wide[:, pair * lanes:(pair + 1) * lanes] = chosen
    total = jnp.dot(wide[...], weight_ref[...], preferred_element_type=F32)
    cols = weight_ref.shape[1]
    total = total.reshape(per, 4, 2, 8, cols).sum(axis=2)
    for home in range(4):
        out_ref[0, home] = total[:, home].reshape(per * 8, cols).astype(BF16)


def return_kernel(
    planes, groups, base_out, code_out, base_in, code_in,
    gathered, total, local_sem, base_send, base_recv, plane_send, plane_recv, home_send, home_recv,
):
    z, xh, t, r = position()
    per = planes // groups
    me = (xh * groups + t) * 2 + r
    count = 4 * groups

    def hello(to_z, to_xh, to_t, to_r):
        pl.semaphore_signal(
            pltpu.get_barrier_semaphore(),
            inc=1,
            device_id=(to_z * 2 + to_xh, to_t, to_r),
            device_id_type=MESH,
        )

    loop(1, planes, lambda d: hello((z + d) % planes, xh, t, r))

    def place_of(j):
        other = (me + j) % count
        return other // (2 * groups), (other // 2) % groups, other % 2

    def hello_plane(j):
        to_xh, to_t, to_r = place_of(j)
        hello(z, to_xh, to_t, to_r)

    loop(1, count, hello_plane)
    stays = (z // per == t).astype(jnp.int32)

    def hello_source(j):
        @pl.when(jnp.logical_not(jnp.logical_and(z // per == t, z % per == j)))
        def _():
            hello(t * per + j, xh, z // per, r)

    for j in range(per):
        hello_source(j)

    def base_copy(d):
        to = (z + d) % planes
        return push(base_out.at[to], base_in.at[z], base_send.at[d], base_recv.at[d], to, xh, t, r)

    def plane_copy(j):
        to_xh, to_t, to_r = place_of(j)
        return push(
            code_out.at[to_t, to_xh * 2 + to_r], gathered.at[me],
            plane_send.at[j], plane_recv.at[j], z, to_xh, to_t, to_r,
        )

    def home_copy(i):
        return push(
            total.at[pl.ds(i * 8, 8), :], code_in.at[z % per],
            home_send.at[i], home_recv.at[z % per], t * per + i, xh, z // per, r,
        )

    def home_arrival(j):
        return push(
            total.at[pl.ds(j * 8, 8), :], code_in.at[j],
            home_send.at[j], home_recv.at[j], t * per + j, xh, z // per, r,
        )

    own_base = pltpu.make_async_copy(base_out.at[z], base_in.at[z], local_sem.at[0])
    own_code = pltpu.make_async_copy(code_out.at[t, xh * 2 + r], gathered.at[me], local_sem.at[1])
    own_base.start()
    own_code.start()
    pl.semaphore_wait(
        pltpu.get_barrier_semaphore(), (planes - 1) + (count - 1) + per - stays
    )
    loop(1, count, lambda j: plane_copy(j).start())
    loop(1, planes, lambda d: base_copy(d).start())
    own_code.wait()
    loop(1, count, lambda j: plane_copy(j).wait())

    def add(j, running):
        return running + gathered[j].astype(F32)

    total[...] = lax.fori_loop(0, count, add, jnp.zeros(total.shape, F32))
    for i in range(per):
        stay = jnp.logical_and(z // per == t, z % per == i)

        @pl.when(jnp.logical_not(stay))
        def _():
            home_copy(i).start()

        @pl.when(stay)
        def _():
            code_in[i] = total[i * 8:(i + 1) * 8, :]

    own_base.wait()
    loop(1, planes, lambda d: base_copy(d).wait())
    for i in range(per):
        stay = jnp.logical_and(z // per == t, z % per == i)

        @pl.when(jnp.logical_not(stay))
        def _():
            home_copy(i).wait_send()
            home_arrival(i).wait_recv()


def shards(base_weight, delta_codes, block_scales, hidden_acts, expert_ids, gate_weights):
    groups = lax.axis_size("tp")
    planes = lax.axis_size("fsdp") // 2
    steps, rows, top = expert_ids.shape
    units = hidden_acts.shape[4]
    width = base_weight.shape[2]
    narrow = delta_codes.shape[2]
    block_count = block_scales.shape[2]
    z, xh, t, r = position()
    capacity = 2
    slot_count = rows * top
    per = planes // groups

    flat_ids = expert_ids.reshape(steps, slot_count)
    slot_index = jnp.arange(slot_count, dtype=jnp.int32)
    earlier = (flat_ids[:, :, None] == flat_ids[:, None, :]) & (
        slot_index[None, None, :] < slot_index[None, :, None]
    )
    order = jnp.sum(earlier.astype(jnp.int32), axis=2)
    select = (
        flat_ids[:, None, None, :] == jnp.arange(planes, dtype=jnp.int32)[None, :, None, None]
    ) & (order[:, None, None, :] == jnp.arange(capacity, dtype=jnp.int32)[None, None, :, None])
    gated = (hidden_acts.astype(F32) * gate_weights[..., None, None]).astype(BF16)
    packed = jnp.einsum(
        "secj,sjph->epsch",
        select.astype(BF16),
        gated.reshape(steps, slot_count, 2, units),
        preferred_element_type=F32,
    ).astype(BF16).reshape(planes, 8, units)
    scales = block_scales.reshape(block_count)
    scale_high = lax.reduce_precision(scales, 8, 7)
    scale_rows = jnp.stack([scale_high, scales - scale_high]).astype(BF16)
    scale_rows = jnp.pad(scale_rows, ((0, 6), (0, units - block_count)))
    disp = jnp.concatenate(
        [packed, jnp.broadcast_to(scale_rows[None], (planes, 8, units))], axis=1
    )
    quarters = (
        gated.reshape(steps, rows, 2, 2, 2, 2, 2, 64)
        .transpose(5, 6, 3, 4, 0, 1, 2, 7)
        .reshape(4, 32, 128)
    )
    tags = expert_ids.reshape(steps, rows, 2, 2, 2).transpose(4, 0, 1, 3, 2).reshape(16, 4)
    tags = jnp.pad(tags.astype(BF16)[:, :, None], ((0, 0), (0, 0), (0, 7))).reshape(16, 1, 32)
    tags = jnp.where((jnp.arange(4) == xh * 2 + r)[None, :, None], tags, 0.0).reshape(1, 16, 128)
    quarters = jnp.concatenate([quarters, jnp.broadcast_to(tags, (4, 16, 128))], axis=1)

    dma = pltpu.SemaphoreType.DMA
    vmem = pl.BlockSpec(memory_space=pltpu.VMEM)
    anywhere = pl.BlockSpec(memory_space=pl.ANY)
    half = planes // 2

    def spread_body(*refs):
        spread_kernel(planes, groups, *refs)

    slots, ring, weights, swapped = pl.pallas_call(
        spread_body,
        out_shape=(
            jax.ShapeDtypeStruct((groups, planes, 16, 128), BF16),
            jax.ShapeDtypeStruct((planes, 144, 128), BF16),
            jax.ShapeDtypeStruct((2 * groups, units, width // groups), BF16),
            jax.ShapeDtypeStruct((2, planes, 64, narrow), BF16),
        ),
        in_specs=[vmem, vmem, anywhere, anywhere],
        out_specs=(vmem, vmem, anywhere, anywhere),
        scratch_shapes=[
            pltpu.VMEM((4, 48, 128), BF16),
            dma((4,)),
            dma((4,)), dma((4,)),
            dma((planes,)), dma((planes,)),
            dma((groups,)), dma((groups,)),
            dma((2 * groups,)), dma((2 * groups,)),
            dma, dma, dma, dma,
            dma((half,)), dma((half,)), dma((half,)), dma((half,)),
        ],
        compiler_params=pltpu.CompilerParams(
            collective_id=0, has_side_effects=True, vmem_limit_bytes=32 << 20
        ),
    )(disp, quarters, base_weight.reshape(units, width), delta_codes.reshape(planes, 2, 64, narrow))

    held_scales = lax.dynamic_index_in_dim(slots, t, 0, keepdims=False)[:, 8:10, :block_count].astype(F32)
    held_scales = held_scales[:, 0] + held_scales[:, 1]
    column = (2 * z + jnp.arange(2, dtype=jnp.int32)[:, None]) * narrow + jnp.arange(narrow, dtype=jnp.int32)[None, :]
    spot = (column // (width // block_count))[:, None, :] == jnp.arange(block_count, dtype=jnp.int32)[None, :, None]
    column_scales = jnp.einsum(
        "eb,xbc->xec", held_scales, spot.astype(F32), precision=lax.Precision.HIGHEST
    )
    scaled = (swapped.astype(F32) * column_scales[:, :, None, :]).astype(BF16)
    scaled = jnp.pad(scaled, ((0, 0), (0, 0), (0, 0), (0, 128 - narrow)))
    scaled = jnp.concatenate([scaled[0], scaled[1]], axis=2).reshape(planes * 64, 256)
    code_out = pl.pallas_call(
        lambda *refs: code_kernel(per, *refs),
        grid=(groups,),
        out_shape=jax.ShapeDtypeStruct((groups, 4, per * 8, 256), BF16),
        in_specs=[
            pl.BlockSpec((per, 144, 128), lambda g: (g, 0, 0)),
            pl.BlockSpec((planes * 64, 256), lambda g: (0, 0)),
        ],
        out_specs=pl.BlockSpec((1, 4, per * 8, 256), lambda g: (g, 0, 0, 0)),
        scratch_shapes=[pltpu.VMEM((per * 64, planes * 64), BF16)],
        compiler_params=pltpu.CompilerParams(vmem_limit_bytes=32 << 20),
    )(ring, scaled)

    acts = (
        slots[:, :, :8, :]
        .reshape(groups, planes, 2, 4, units)
        .transpose(1, 3, 0, 2, 4)
        .reshape(planes * 4, groups * 2 * units)
    )
    projected = jnp.dot(
        acts, weights.reshape(groups * 2 * units, width // groups), preferred_element_type=F32
    ).astype(BF16)
    lines = 4 * (width // groups) // 128
    base_out = jnp.pad(projected.reshape(planes, lines, 128), ((0, 0), (0, 32 - lines), (0, 0)))

    def return_body(*refs):
        return_kernel(planes, groups, *refs)

    base_in, code_in = pl.pallas_call(
        return_body,
        out_shape=(
            jax.ShapeDtypeStruct((planes, 32, 128), BF16),
            jax.ShapeDtypeStruct((per, 8, 256), F32),
        ),
        in_specs=[vmem, vmem],
        out_specs=(vmem, vmem),
        scratch_shapes=[
            pltpu.VMEM((4 * groups, per * 8, 256), BF16),
            pltpu.VMEM((per * 8, 256), F32),
            dma((2,)),
            dma((planes,)), dma((planes,)),
            dma((4 * groups,)), dma((4 * groups,)),
            dma((per,)), dma((per,)),
        ],
        compiler_params=pltpu.CompilerParams(
            collective_id=1, has_side_effects=True, vmem_limit_bytes=32 << 20
        ),
    )(base_out, code_out)

    back = base_in[:, :lines].reshape(planes, steps, capacity, width // groups)
    row_select = select.reshape(steps, planes, capacity, rows, top).astype(F32).sum(axis=4).astype(BF16)
    mixed = jnp.einsum("secn,escd->snd", row_select, back, preferred_element_type=F32)
    coded = (
        code_in.reshape(per, steps, rows, 2, 128)[..., :narrow]
        .transpose(1, 2, 0, 3, 4)
        .reshape(steps, rows, width // groups)
    )
    return (mixed + coded).astype(BF16)


def solution(mesh):
    placed = (
        P("fsdp", "tp", None),
        P(None, ("tp", "rep"), "fsdp"),
        P("fsdp", "tp", None),
        P(None, ("fsdp", "rep"), None, None, "tp"),
        P(None, ("fsdp", "rep"), None),
        P(None, ("fsdp", "rep"), None),
    )
    return jax.shard_map(
        shards,
        mesh=mesh,
        in_specs=placed,
        out_specs=P(None, ("fsdp", "rep"), "tp"),
        check_vma=False,
    )
```

time: 398 us -> 166 us (0.42)
  the two profiles are of different devices: /device:TPU:24 before, /device:TPU:86 now
where the time goes in v1:
time: 166 us; the launch traced here: 165 us
  Pallas kernels  149 us (90%)
  local copies, waits for them, and re-layouts  8.76 us (5%)
  matrix products  3.87 us (2%)
  other arithmetic  3.27 us (2%)
    pallas_call x1, Pallas kernels, shards(): pl.pallas_call(spread_body, out_shape=(jax.ShapeDtypeStruct((groups, plan...  86.4 us
    pallas_call x1, Pallas kernels, shards(): pl.pallas_call(return_body, out_shape=(jax.ShapeDtypeStruct((planes, 32,...  55.6 us
    pallas_call x1, Pallas kernels, shards(): pl.pallas_call(lambda *refs: code_kernel(per, *refs), grid=(groups,), out...  7.08 us
    unnamed x7, local copies, waits for them, and re-layouts  5.27 us

profile of v1, /device:TPU:86, one launch (start us, length us, event | category | flops | bytes accessed | tf_op | source)
XLA Modules:
  0.0 165.2 jit_solution(11415398944457527436)
XLA Ops:
  0.0 0.1 broadcast_in_dim.33
  0.1 0.1 broadcast_in_dim.54
  0.2 0.1 and_select_fusion
  0.3 0.8 eq.93
  1.0 0.7 reduce-precision_convert_fusion
  1.7 0.2 convert_reduce_fusion.1
  1.9 0.1 eq.97
  2.0 0.8 iota_compare_fusion.3
  2.8 0.1 convert_reduce_fusion
  2.9 0.8 copy.27
  3.7 0.1 convert_element_type.84
  3.8 0.1 copy.30
  3.9 0.1 broadcast_in_dim.58
  4.0 0.9 multiply_convert_fusion.1
  4.9 0.1 fusion
  5.0 0.1 copy.25
  5.1 0.1 reshape.199
  5.2 0.1 copy.47
  5.3 0.1 reshape.200
  5.4 0.0 copy-start.1
  5.4 1.5 copy-done.1
  6.9 0.0 copy-start.2
  6.9 1.2 copy-done.2
  8.1 86.4 %shard_map.64 = (bf16[8,32,16,128]{3,2,1,0:T(8,128)(2,1)S(1)}, bf16[32,144,128]{2,1,0:T(8,128)(2,1)S(1)}, bf16[16,128,896]{2,1,0:T(8,128)(2,1)S(1)}, bf16[2,32,64,112]{3,2,1,0:T(8,128)(2,1)S(1)}) custom-call(bf16[32,16,128]{2,1,0:T(8,128)(2,1)S(1)} %pad_maximum_fusion.1.refs_0_, bf16[4,48,128]{2,1,0:T(8,128)(2,1)S(1)} %pad_maximum_fusion.2.refs_1_, ...), custom_call_target="tpu_custom_call" | custom-call | tf_op jit(solution)/shard_map/pallas_call | solution.py:356
  94.5 0.0 copy-start
  94.6 1.8 %copy-done = bf16[16,128,896]{2,1,0:T(8,128)(2,1)} copy-done((bf16[16,128,896]{2,1,0:T(8,128)(2,1)}, bf16[16,128,896]{2,1,0:T(8,128)(2,1)S(1)}, u32[]{:S(2)}) %copy-start) | copy-done | bytes 3670040
  96.3 0.1 slice.24
  96.5 0.6 copy.46
  97.1 0.4 reshape.204
  97.5 2.8 %convolution_convert_fusion = bf16[128,896]{1,0:T(8,128)(2,1)S(1)} fusion(bf16[128,2048]{1,0:T(8,128)(2,1)S(1)} %reshape.204, bf16[2048,896]{1,0:T(8,128)(2,1)} %bitcast.53), kind=kOutput, calls=%fused_computation.1 | convolution fusion | flops 469876736 | bytes 4423680 | tf_op jit(solution)/shard_map/dot_general | solution.py:410
  100.2 0.1 convolution_bitcast_fusion
  100.4 0.3 multiply_convert_fusion
  100.7 0.3 pad_slice_fusion.1
  101.0 0.1 pad_maximum_fusion.refs_1_
  101.1 7.1 %shard_map.65.refs_1_ = bf16[8,4,32,256]{3,2,1,0:T(8,128)(2,1)S(1)} custom-call(bf16[32,144,128]{2,1,0:T(8,128)(2,1)S(1)} %get-tuple-element.13.refs_0_, bf16[2048,256]{1,0:T(8,128)(2,1)S(1)} %pad_maximum_fusion.refs_1_), custom_call_target="tpu_custom_call" | custom-call | tf_op jit(solution)/shard_map/pallas_call | solution.py:391
  108.2 0.2 reshape.206
  108.5 55.6 %shard_map.66 = (bf16[32,32,128]{2,1,0:T(8,128)(2,1)S(1)}, f32[4,8,256]{2,1,0:T(8,128)S(1)}) custom-call(bf16[32,32,128]{2,1,0:T(8,128)(2,1)S(1)} %pad.18.refs_0_, bf16[8,4,32,256]{3,2,1,0:T(8,128)(2,1)S(1)} %shard_map.65.refs_1_), custom_call_target="tpu_custom_call" | custom-call | tf_op jit(solution)/shard_map/pallas_call | solution.py:419
  164.1 0.1 reshape.207
  164.3 0.1 reshape.209
  164.4 0.8 fusion.2
  (23 shorter events, 0.3 us)
Async XLA Ops:
  5.4 1.5 copy-start.1
  6.9 1.2 copy-start.2
  94.5 1.8 %copy-start = (bf16[16,128,896]{2,1,0:T(8,128)(2,1)}, bf16[16,128,896]{2,1,0:T(8,128)(2,1)S(1)}, u32[]{:S(2)}) copy-start(bf16[16,128,896]{2,1,0:T(8,128)(2,1)S(1)} %get-tuple-element.12) | copy-start | bytes 11010052

commit v2 on v0

v2 whole, which is shorter than its diff:
```python
import jax
import jax.numpy as jnp
from jax import lax
from jax.experimental import pallas as pl
from jax.experimental.pallas import tpu as pltpu
from jax.sharding import PartitionSpec as P

MESH = pl.DeviceIdType.MESH
BF16 = jnp.bfloat16
F32 = jnp.float32


def position():
    f, t, r = lax.axis_index("fsdp"), lax.axis_index("tp"), lax.axis_index("rep")
    return f // 2, f % 2, t, r


def push(src, dst, send_sem, recv_sem, z, xh, t, r):
    return pltpu.make_async_remote_copy(
        src_ref=src,
        dst_ref=dst,
        send_sem=send_sem,
        recv_sem=recv_sem,
        device_id=(z * 2 + xh, t, r),
        device_id_type=MESH,
    )


def loop(low, high, body):
    def step(i, carry):
        body(i)
        return carry

    lax.fori_loop(low, high, step, jnp.int32(0))


def iota(shape, axis):
    return lax.broadcasted_iota(jnp.int32, shape, axis)


def one_hot(condition):
    return jnp.where(condition, 1.0, 0.0).astype(BF16)


STRIDE = 2


def resync_kernel(
    planes, groups, hidden, ids, gate_weights, scales, base, codes,
    base_in, code_in,
    scale_rows, disp, quarters, quad, slots, ring, weights, swapped, column_scales, wide_weights, wide,
    acts, base_out, code_out, gathered, total,
    local_sem, quad_send, quad_recv, disp_send, disp_recv, tp_send, tp_recv,
    w_send, w_recv, pair_send, pair_recv, code_send, code_recv,
    right_send, right_recv, left_send, left_recv,
    base_send, base_recv, plane_send, plane_recv, home_send, home_recv,
):
    z, xh, t, r = position()
    home = xh * 2 + r
    place = xh * groups + t
    me = place * 2 + r
    count = 4 * groups
    per = planes // groups
    half_units = base.shape[0] // 2
    width = weights.shape[2]
    narrow = codes.shape[3]
    lanes = 128

    def hello(to_z, to_xh, to_t, to_r):
        pl.semaphore_signal(
            pltpu.get_barrier_semaphore(),
            inc=1,
            device_id=(to_z * 2 + to_xh, to_t, to_r),
            device_id_type=MESH,
        )

    def place_of(j):
        other = (me + j) % count
        return other // (2 * groups), (other // 2) % groups, other % 2

    def hello_plane(j):
        to_xh, to_t, to_r = place_of(j)
        hello(z, to_xh, to_t, to_r)

    def stays(i):
        return jnp.logical_and(z // per == t, z % per == i)

    loop(1, planes, lambda d: hello((z + d) % planes, xh, t, r))
    loop(1, count, hello_plane)
    for j in range(per):
        @pl.when(jnp.logical_not(stays(j)))
        def _():
            hello(t * per + j, xh, z // per, r)

    def quad_copy(i):
        to = (home + i) % 4
        return push(quarters.at[to], quad.at[home], quad_send.at[i], quad_recv.at[i], z, to // 2, t, to % 2)

    def disp_copy(d):
        to = (z + d) % planes
        return push(disp.at[to], slots.at[z], disp_send.at[d], disp_recv.at[d], to, xh, t, r)

    def tp_copy(j):
        return push(acts.at[t], acts.at[t], tp_send.at[j], tp_recv.at[j], z, xh, (t + j) % groups, r)

    rows_here = pl.ds(pl.multiple_of(r * half_units, half_units), half_units)

    def w_columns(to_t):
        return pl.ds(pl.multiple_of(to_t * width, lanes), width)

    def w_copy(j):
        to = (place + j) % (2 * groups)
        return push(
            base.at[rows_here, w_columns(to % groups)], weights.at[place, rows_here, :],
            w_send.at[j], w_recv.at[j], z, to // groups, to % groups, r,
        )

    def pair_copy(j):
        block = weights.at[(place + 2 * groups - j) % (2 * groups), rows_here, :]
        return push(block, block, pair_send.at[j], pair_recv.at[j], z, xh, t, 1 - r)

    def code_copy():
        return push(codes.at[:, 1 - xh], swapped.at[xh], code_send, code_recv, z, 1 - xh, t, r)

    def right_block(o):
        return ring.at[(z - o + planes) % planes]

    def left_block(o):
        return ring.at[(z + o) % planes]

    def right_seed(d):
        return push(ring.at[z], ring.at[z], right_send.at[d], right_recv.at[d], (z + d) % planes, xh, t, r)

    def left_seed(d):
        return push(ring.at[z], ring.at[z], left_send.at[d], left_recv.at[d], (z + planes - d) % planes, xh, t, r)

    def right_next(o):
        return push(
            right_block(o), right_block(o), right_send.at[o + STRIDE], right_recv.at[o + STRIDE],
            (z + STRIDE) % planes, xh, t, r,
        )

    def left_next(o):
        return push(
            left_block(o), left_block(o), left_send.at[o + STRIDE], left_recv.at[o + STRIDE],
            (z + planes - STRIDE) % planes, xh, t, r,
        )

    def right_wait(o):
        push(right_block(o), right_block(o), right_send.at[o], right_recv.at[o], z ^ 1, xh, t, r).wait_recv()

    def left_wait(o):
        push(left_block(o), left_block(o), left_send.at[o], left_recv.at[o], z ^ 1, xh, t, r).wait_recv()

    right_last = planes // 2
    left_last = planes - 1 - right_last

    def ring_steps(low, high):
        def step(o):
            right_wait(o)
            right_next(o).start()
            left_wait(o)
            left_next(o).start()

        loop(low, high, step)

    def base_copy(d):
        to = (z + d) % planes
        return push(base_out.at[to], base_in.at[z], base_send.at[d], base_recv.at[d], to, xh, t, r)

    def plane_copy(j):
        to_xh, to_t, to_r = place_of(j)
        return push(
            code_out.at[to_t, to_xh * 2 + to_r], gathered.at[me],
            plane_send.at[j], plane_recv.at[j], z, to_xh, to_t, to_r,
        )

    def home_copy(i):
        return push(
            total.at[pl.ds(i * 8, 8), :], code_in.at[z % per],
            home_send.at[i], home_recv.at[z % per], t * per + i, xh, z // per, r,
        )

    def home_arrival(j):
        return push(
            total.at[pl.ds(j * 8, 8), :], code_in.at[j],
            home_send.at[j], home_recv.at[j], t * per + j, xh, z // per, r,
        )

    own_w = pltpu.make_async_copy(
        base.at[rows_here, w_columns(t)], weights.at[place, rows_here, :], local_sem.at[0]
    )
    own_codes = pltpu.make_async_copy(codes.at[:, xh], swapped.at[xh], local_sem.at[1])
    own_w.start()
    own_codes.start()

    square = (lanes, lanes)
    def column_of(values):
        tall = jnp.broadcast_to(values[:, None, :], (8, 16, 8)).reshape(lanes, 8)
        mine = iota((lanes, 8), 1) == iota((lanes, 8), 0) // 2 % 8
        return jnp.sum(jnp.where(mine, tall, 0.0), axis=1, keepdims=True)

    gated = (hidden[...].astype(F32) * column_of(gate_weights[...])).astype(BF16)
    names_column = jnp.broadcast_to(column_of(ids[...].astype(F32)), square)
    row, col = iota(square, 0), iota(square, 1)
    wanted = (
        ((row // 4) % 2 * 4 + row % 4) * 16 + (row // 32 % 2) * 8 + (row // 16 % 2) * 4
        + (row // 8 % 2) * 2 + row // 64
    )
    sorted_rows = jnp.dot(one_hot(col == wanted), gated, preferred_element_type=F32).astype(BF16)
    for half in range(2):
        low = sorted_rows[half * 64:half * 64 + 32, :]
        high = sorted_rows[half * 64 + 32:half * 64 + 64, :]
        quarters[half * 2, 0:32, :] = jnp.concatenate([low[:, :64], high[:, :64]], axis=1)
        quarters[half * 2 + 1, 0:32, :] = jnp.concatenate([low[:, 64:], high[:, 64:]], axis=1)
    named = jnp.sum(jnp.where(row == col, names_column, 0.0), axis=0, keepdims=True)
    tag_shape = (16, lanes)
    tag_row, tag_col = iota(tag_shape, 0), iota(tag_shape, 1)
    tag_at = (
        ((tag_row // 4) % 2 * 4 + tag_row % 4 == tag_col // 16)
        & (tag_row // 8 == tag_col // 2 % 2) & (tag_col % 2 == 0)
    )
    tag_values = jnp.where(tag_at, jnp.broadcast_to(named, tag_shape), 0.0).astype(BF16)
    tag_lane = home * 32 + ((row // 4 % 2) * 2 + row // 8 % 2) * 8
    tags = jnp.dot(tag_values, one_hot(col == tag_lane), preferred_element_type=F32).astype(BF16)
    for i in range(4):
        quarters[i, 32:48, :] = tags
    same = (
        (names_column == named) & (row < col) & (row % 2 == col % 2) & (row // 64 == col // 64)
    )
    order = jnp.sum(jnp.where(same, 1.0, 0.0), axis=0, keepdims=True)
    pack_shape = (planes * 8, lanes)
    pack_row, pack_col = iota(pack_shape, 0), iota(pack_shape, 1)
    picked = (
        (jnp.broadcast_to(named, pack_shape) == (pack_row // 8).astype(F32))
        & (jnp.broadcast_to(order, pack_shape) == (pack_row % 2).astype(F32))
        & (pack_row // 2 % 2 == pack_col // 64) & (pack_row // 4 % 2 == pack_col % 2)
    )
    packed = jnp.dot(one_hot(picked), gated, preferred_element_type=F32).reshape(planes, 8, lanes)
    blocks = scales.shape[1]
    high = scales[...].astype(BF16).astype(F32)
    scale_rows[...] = jnp.zeros(scale_rows.shape, F32)
    scale_rows[0:1, :blocks] = high
    scale_rows[1:2, :blocks] = scales[...] - high
    disp[...] = jnp.concatenate(
        [packed, jnp.broadcast_to(scale_rows[...][None], (planes, 8, lanes))], axis=1
    ).astype(BF16)
    wide_weights[...] = jnp.zeros(wide_weights.shape, BF16)
    pl.semaphore_wait(
        pltpu.get_barrier_semaphore(),
        (planes - 1) + (count - 1) + per - (z // per == t).astype(jnp.int32),
    )

    for i in range(1, 4):
        quad_copy(i).start()
    loop(1, 2 * groups, lambda j: w_copy(j).start())
    code_copy().start()
    quad[home] = quarters[home]
    for i in range(1, 4):
        quad_copy(i).wait()
    for i in range(4):
        ring[z, i * 32:(i + 1) * 32, :] = quad[i, :32, :]
    ring[z, 128:, :] = quad[0, 32:, :] + quad[1, 32:, :] + quad[2, 32:, :] + quad[3, 32:, :]
    for d in range(1, STRIDE + 1):
        right_seed(d).start()
        left_seed(d).start()
    loop(1, planes, lambda d: disp_copy(d).start())
    slots[z] = disp[z]

    def code_group(index):
        g = (z // per + ((index + 1) // 2) * (2 * (index % 2) - 1) + groups) % groups
        block = ring[pl.ds(g * per, per)]
        rows = per * 64
        tag_block = block[:, 128:, :].reshape(per * 16, lanes)
        lane_in, lane_out = iota((lanes, 4 * lanes), 0), iota((lanes, 4 * lanes), 1)
        names = []
        for h in range(4):
            pick = one_hot(lane_in == h * 32 + (lane_out // lanes) * 8)
            spread = jnp.dot(tag_block, pick, preferred_element_type=F32)
            names.append(spread.reshape(per, 1, 16, 4 * lanes))
        names = jnp.concatenate(names, axis=1).reshape(rows, 4 * lanes)
        upper = jnp.where(iota((rows, 4 * lanes), 1) % lanes >= 64, 1.0, 0.0)
        names = (names - upper).astype(BF16)
        lane_in, lane_out = iota((lanes, 2 * lanes), 0), iota((lanes, 2 * lanes), 1)
        double = one_hot(lane_in == (lane_out // lanes) * 64 + lane_out % 64)
        parts = block[:, :128, :].reshape(per, 4, 2, 16, lanes)
        values, tagged = [], []
        for m in range(2):
            both = jnp.dot(
                parts[:, :, m].reshape(rows, lanes), double, preferred_element_type=F32
            ).astype(BF16)
            for j in range(2):
                values.append(both[:, j * lanes:(j + 1) * lanes])
                tagged.append(names[:, (m * 2 + j) * lanes:(m * 2 + j + 1) * lanes])
        for pair in range(planes // 2):
            chosen = jnp.zeros((rows, lanes), BF16)
            for value, name in zip(values, tagged):
                chosen = jnp.where(name == jnp.asarray(2.0 * pair, BF16), value, chosen)
            wide[:, pair * lanes:(pair + 1) * lanes] = chosen
        result = jnp.dot(wide[...], wide_weights[...], preferred_element_type=F32)
        cols = wide_weights.shape[1]
        result = result.reshape(per, 4, 2, 8, cols).sum(axis=2)
        for h in range(4):
            code_out[g, h] = result[:, h].reshape(per * 8, cols).astype(BF16)
        for h in range(4):
            to = ((h // 2) * groups + g) * 2 + h % 2
            leaves = to != me

            @pl.when(leaves)
            def _():
                plane_copy((to - me + count) % count).start()

            @pl.when(jnp.logical_not(leaves))
            def _():
                gathered[me] = code_out[g, h]

    ring_steps(1, 9)
    loop(1, planes, lambda d: disp_copy(d).wait())
    acts[t] = slots[...].astype(F32)[:, :8, :].reshape(planes * 8, lanes).astype(BF16)
    loop(1, groups, lambda j: tp_copy(j).start())
    ring_steps(9, 10)

    own_codes.wait()
    code_copy().wait()
    spot_in, spot_out = iota((lanes, 2 * lanes), 0), iota((lanes, 2 * lanes), 1)
    column = (2 * z + spot_out // lanes) * narrow + spot_out % lanes
    spot = one_hot((column // lanes == spot_in) & (spot_out % lanes < narrow))
    spread = jnp.dot(
        slots[...].reshape(planes * 16, lanes), spot, preferred_element_type=F32
    ).reshape(planes, 16, 2 * lanes)
    column_scales[...] = spread[:, 8:9, :] + spread[:, 9:10, :]

    def scale_expert(e):
        at = pl.ds(pl.multiple_of(e * 64, 64), 64)
        for x in range(2):
            scale = column_scales[e, :, x * lanes:x * lanes + narrow]
            wide_weights[at, x * lanes:x * lanes + narrow] = (
                swapped[x, e].astype(F32) * scale
            ).astype(BF16)

    loop(0, planes, scale_expert)
    ring_steps(10, 11)
    loop(0, 1, code_group)
    ring_steps(11, 12)
    own_w.wait()
    pair_copy(0).start()

    def pass_on(j):
        w_copy(j).wait_recv()
        pair_copy(j).start()

    loop(1, 2 * groups, pass_on)
    ring_steps(12, 13)
    loop(1, 3, code_group)
    ring_steps(13, left_last - STRIDE + 1)
    for o in range(left_last - STRIDE + 1, right_last - STRIDE + 1):
        right_wait(o)
        right_next(o).start()

    loop(1, groups, lambda j: tp_copy(j).wait())
    loop(0, 2 * groups, lambda j: pair_copy(j).wait())
    left = jnp.concatenate([acts[g] for g in range(groups)], axis=1)
    first = iota((planes, 8, lanes), 1) < 4
    lines = []
    for c in range(0, width, 2 * lanes):
        wide_cols = min(2 * lanes, width - c)
        zero, one = [
            jnp.dot(
                left,
                weights[p * groups:(p + 1) * groups, :, c:c + wide_cols].reshape(groups * lanes, wide_cols),
                preferred_element_type=F32,
            ).reshape(planes, 8, wide_cols)
            for p in range(2)
        ]
        blank = jnp.zeros((planes, 8, lanes), F32)
        zero_next, one_next = (zero[:, :, lanes:], one[:, :, lanes:]) if wide_cols > lanes else (blank, blank)
        stay = jnp.where(first, zero[:, :, :lanes], one_next)
        move = jnp.where(first, zero_next, one[:, :, :lanes])
        lines.append(stay + pltpu.roll(move, 4, 1))
    base_out[...] = jnp.concatenate(lines, axis=1).astype(BF16)
    loop(1, planes, lambda d: base_copy(d).start())
    base_in[z] = base_out[z]

    loop(3, 5, code_group)
    for o in range(right_last - STRIDE + 1, right_last + 1):
        right_wait(o)
    for o in range(left_last - STRIDE + 1, left_last + 1):
        left_wait(o)
    loop(5, groups, code_group)

    loop(1, count, lambda j: plane_copy(j).wait())

    def add(j, running):
        return running + gathered[j].astype(F32)

    total[...] = lax.fori_loop(0, count, add, jnp.zeros(total.shape, F32))
    for i in range(per):
        @pl.when(jnp.logical_not(stays(i)))
        def _():
            home_copy(i).start()

        @pl.when(stays(i))
        def _():
            code_in[i] = total[i * 8:(i + 1) * 8, :]

    loop(1, 2 * groups, lambda j: w_copy(j).wait_send())
    for d in range(1, STRIDE + 1):
        right_seed(d).wait_send()
        left_seed(d).wait_send()
    loop(1, right_last - STRIDE + 1, lambda o: right_next(o).wait_send())
    loop(1, left_last - STRIDE + 1, lambda o: left_next(o).wait_send())
    loop(1, planes, lambda d: base_copy(d).wait())
    for i in range(per):
        @pl.when(jnp.logical_not(stays(i)))
        def _():
            home_copy(i).wait_send()
            home_arrival(i).wait_recv()


def shards(base_weight, delta_codes, block_scales, hidden_acts, expert_ids, gate_weights):
    groups = lax.axis_size("tp")
    planes = lax.axis_size("fsdp") // 2
    steps, rows, top = expert_ids.shape
    units = hidden_acts.shape[4]
    width = base_weight.shape[2]
    narrow = delta_codes.shape[2]
    block_count = block_scales.shape[2]
    capacity = 2
    slot_count = rows * top
    per = planes // groups
    total_slots = steps * slot_count

    dma = pltpu.SemaphoreType.DMA
    vmem = pl.BlockSpec(memory_space=pltpu.VMEM)
    outside = pl.BlockSpec(memory_space=pltpu.HBM)
    count = 4 * groups

    def body(*refs):
        resync_kernel(planes, groups, *refs)

    base_in, code_in = pl.pallas_call(
        body,
        out_shape=(
            jax.ShapeDtypeStruct((planes, 32, 128), BF16),
            jax.ShapeDtypeStruct((per, 8, 256), F32),
        ),
        in_specs=[vmem, vmem, vmem, vmem, outside, outside],
        out_specs=(vmem, vmem),
        scratch_shapes=[
            pltpu.VMEM((8, 128), F32),
            pltpu.VMEM((planes, 16, 128), BF16),
            pltpu.VMEM((4, 48, 128), BF16),
            pltpu.VMEM((4, 48, 128), BF16),
            pltpu.VMEM((planes, 16, 128), BF16),
            pltpu.VMEM((planes, 144, 128), BF16),
            pltpu.VMEM((2 * groups, units, width // groups), BF16),
            pltpu.VMEM((2, planes, 64, narrow), BF16),
            pltpu.VMEM((planes, 1, 256), F32),
            pltpu.VMEM((planes * 64, 256), BF16),
            pltpu.VMEM((per * 64, planes * 64), BF16),
            pltpu.VMEM((groups, planes * 8, units), BF16),
            pltpu.VMEM((planes, 32, 128), BF16),
            pltpu.VMEM((groups, 4, per * 8, 256), BF16),
            pltpu.VMEM((count, per * 8, 256), BF16),
            pltpu.VMEM((per * 8, 256), F32),
            dma((2,)),
            dma((4,)), dma((4,)),
            dma((planes,)), dma((planes,)),
            dma((groups,)), dma((groups,)),
            dma((2 * groups,)), dma((2 * groups,)),
            dma((2 * groups,)), dma((2 * groups,)),
            dma, dma,
            dma((planes,)), dma((planes,)), dma((planes,)), dma((planes,)),
            dma((planes,)), dma((planes,)),
            dma((count,)), dma((count,)),
            dma((per,)), dma((per,)),
        ],
        compiler_params=pltpu.CompilerParams(
            collective_id=0, has_side_effects=True, vmem_limit_bytes=40 << 20
        ),
    )(
        hidden_acts.reshape(total_slots * 2, units),
        expert_ids.reshape(steps * rows, top),
        gate_weights.reshape(steps * rows, top),
        block_scales.reshape(1, block_count),
        base_weight.reshape(units, width),
        delta_codes.reshape(planes, 2, 64, narrow),
    )

    flat_ids = expert_ids.reshape(steps, slot_count)
    slot_index = jnp.arange(slot_count, dtype=jnp.int32)
    earlier = (flat_ids[:, :, None] == flat_ids[:, None, :]) & (
        slot_index[None, None, :] < slot_index[None, :, None]
    )
    order = jnp.sum(earlier.astype(jnp.int32), axis=2)
    select = (
        flat_ids[:, None, None, :] == jnp.arange(planes, dtype=jnp.int32)[None, :, None, None]
    ) & (order[:, None, None, :] == jnp.arange(capacity, dtype=jnp.int32)[None, None, :, None])
    row_select = select.reshape(steps, planes, capacity, rows, top).astype(F32).sum(axis=4).astype(BF16)
    blocks = width // groups // 128
    back = base_in[:, :4 * blocks].reshape(planes, blocks, steps, capacity, 128)
    mixed = jnp.einsum("secn,ebscl->snbl", row_select, back, preferred_element_type=F32)
    coded = (
        code_in.reshape(per, steps, rows, 2, 128)[..., :narrow]
        .transpose(1, 2, 0, 3, 4)
        .reshape(steps, rows, width // groups)
    )
    return (mixed.reshape(steps, rows, width // groups) + coded).astype(BF16)


def solution(mesh):
    placed = (
        P("fsdp", "tp", None),
        P(None, ("tp", "rep"), "fsdp"),
        P("fsdp", "tp", None),
        P(None, ("fsdp", "rep"), None, None, "tp"),
        P(None, ("fsdp", "rep"), None),
        P(None, ("fsdp", "rep"), None),
    )
    return jax.shard_map(
        shards,
        mesh=mesh,
        in_specs=placed,
        out_specs=P(None, ("fsdp", "rep"), "tp"),
        check_vma=False,
    )
```

time: 398 us -> 123 us (0.31)
  blocking collectives: 173 us -> 0 us
  Pallas kernels: 0 us -> 115 us
  waiting for transfers between devices: 107 us -> 0 us
  starting transfers between devices: 50.7 us -> 0 us
  local copies, waits for them, and re-layouts: 41.4 us -> 5.92 us
  between operations: 13.3 us -> 0.07 us
  matrix products: 8.22 us -> 0.82 us
    all_to_all x2 -> x0, blocking collectives: 173 us -> none  [the longest x1 142 us: shards(): lax.all_to_all(delta_codes, 'fsdp', split_axis=0, concat_axis=2, tiled=True)]
    pallas_call x0 -> x1, Pallas kernels: none -> 115 us  [shards(): pl.pallas_call(body, out_shape=(jax.ShapeDtypeStruct((planes, 32, 128), B...]
    all_to_all x3 -> x0, waiting for transfers between devices: 64.8 us -> none  [the longest x2 39.8 us: shards(): lax.all_to_all(totals.astype(jnp.bfloat16), 'fsdp', split_axis=0, concat_...]
    all_to_all x3 -> x0, starting transfers between devices: 50.6 us -> none  [the longest x2 45.2 us: shards(): lax.all_to_all(totals.astype(jnp.bfloat16), 'fsdp', split_axis=0, concat_...]
    unnamed x5 -> x0, waiting for transfers between devices: 42.4 us -> none
    unnamed x16 -> x14, local copies, waits for them, and re-layouts: 33.6 us -> 5.51 us
    dot_general x6 -> x1, matrix products: 8.22 us -> 0.82 us  [shards(): jnp.einsum('secn,ebscl->snbl', row_select, back, preferred_element_type=F32)]
  transfers between devices with their start and end apart: 6 -> 0, of which waited for: 3 -> 0; matrix products, arithmetic and copies ran while one was open for 7% -> 0% of each run, Pallas kernels for 0% -> 0%
where the time goes in v2:
time: 123 us; the launch traced here: 122 us
  Pallas kernels  115 us (93%)
  local copies, waits for them, and re-layouts  5.92 us (5%)
    pallas_call x1, Pallas kernels, shards(): pl.pallas_call(body, out_shape=(jax.ShapeDtypeStruct((planes, 32, 128), B...  115 us
    unnamed x14, local copies, waits for them, and re-layouts  5.51 us

profile of v2, /device:TPU:24, one launch (start us, length us, event | category | flops | bytes accessed | tf_op | source)
XLA Modules:
  0.0 122.2 jit_solution(7719743720108229265)
XLA Ops:
  0.0 0.0 copy-start
  0.0 1.5 %copy-done = bf16[1,128,7168]{2,1,0:T(8,128)(2,1)S(1)} copy-done((bf16[1,128,7168]{2,1,0:T(8,128)(2,1)S(1)}, bf16[1,128,7168]{2,1,0:T(8,128)(2,1)}, u32[]{:S(2)}) %copy-start) | copy-done | bytes 1835032
  1.5 0.0 copy-start.1
  1.5 1.2 %copy-done.1 = bf16[64,64,112]{2,1,0:T(8,128)(2,1)S(1)} copy-done((bf16[64,64,112]{2,1,0:T(8,128)(2,1)S(1)}, bf16[64,64,112]{2,1,0:T(8,128)(2,1)}, u32[]{:S(2)}) %copy-start.1) | copy-done | bytes 917528
  2.7 0.0 copy-start.2
  2.7 0.7 copy-done.2
  3.4 0.0 copy-start.4
  3.4 0.8 copy-done.4
  4.2 0.0 copy-start.5
  4.2 0.7 copy-done.5
  4.9 0.0 copy-start.6
  4.9 0.7 copy-done.6
  5.5 0.0 copy-start.3
  5.5 115.0 %shard_map.64 = (bf16[32,32,128]{2,1,0:T(8,128)(2,1)S(1)}, f32[4,8,256]{2,1,0:T(8,128)S(1)}) custom-call(bf16[128,128]{1,0:T(8,128)(2,1)S(1)} %bitcast.28, s32[8,8]{1,0:T(8,128)S(1)} %bitcast.27, f32[8,8]{1,0:T(8,128)S(1)} %bitcast.29, f32[1,56]{1,0:T(1,128)S(1)} %bitcast.30, bf16[128,7168]{1,0:T(8,128)(2,1)S(1)} %bitcast.24, ...), custom_call_target="tpu_custom_call" | custom-call | tf_op jit(solution)/shard_map/pallas_call | solution.py:441
  120.6 0.1 reshape.80
  120.7 0.1 copy.12
  120.8 0.0 copy-done.3
  120.8 0.1 eq.56
  120.9 0.2 convert_reduce_fusion.1
  121.1 0.1 eq.60
  121.2 0.1 iota_compare_fusion
  121.3 0.1 convert_reduce_fusion
  121.4 0.8 fusion.1
  (5 shorter events, 0.1 us)
Async XLA Ops:
  0.0 1.5 %copy-start = (bf16[1,128,7168]{2,1,0:T(8,128)(2,1)S(1)}, bf16[1,128,7168]{2,1,0:T(8,128)(2,1)}, u32[]{:S(2)}) copy-start(bf16[1,128,7168]{2,1,0:T(8,128)(2,1)} %param.6) | copy-start | bytes 5505028
  1.5 1.2 %copy-start.1 = (bf16[64,64,112]{2,1,0:T(8,128)(2,1)S(1)}, bf16[64,64,112]{2,1,0:T(8,128)(2,1)}, u32[]{:S(2)}) copy-start(bf16[64,64,112]{2,1,0:T(8,128)(2,1)} %param.7) | copy-start | bytes 2752516
  2.7 0.7 copy-start.2
  3.4 0.8 copy-start.4
  4.2 0.7 copy-start.5
  4.9 0.7 copy-start.6
  5.5 115.3 %copy-start.3 = (s32[2,4,8]{2,1,0:T(4,128)S(1)}, s32[2,4,8]{2,1,0:T(4,128)}, u32[]{:S(2)}) copy-start(s32[2,4,8]{2,1,0:T(4,128)} %param.10) | copy-start | bytes 772

commit v3 on v2

--- a/solution.py
+++ b/solution.py
@@ -85,7 +85,14 @@
     def stays(i):
         return jnp.logical_and(z // per == t, z % per == i)
 
-    loop(1, planes, lambda d: hello((z + d) % planes, xh, t, r))
+    far = planes // 2
+
+    def hello_both(i):
+        hello((z + far + i) % planes, xh, t, r)
+        hello((z + far - i + planes) % planes, xh, t, r)
+
+    hello((z + far) % planes, xh, t, r)
+    loop(1, far, hello_both)
     loop(1, count, hello_plane)
     for j in range(per):
         @pl.when(jnp.logical_not(stays(j)))
@@ -351,7 +358,6 @@
 
     loop(1, 2 * groups, pass_on)
     ring_steps(12, 13)
-    loop(1, 3, code_group)
     ring_steps(13, left_last - STRIDE + 1)
     for o in range(left_last - STRIDE + 1, right_last - STRIDE + 1):
         right_wait(o)
@@ -381,7 +387,7 @@
     loop(1, planes, lambda d: base_copy(d).start())
     base_in[z] = base_out[z]
 
-    loop(3, 5, code_group)
+    loop(1, 5, code_group)
     for o in range(right_last - STRIDE + 1, right_last + 1):
         right_wait(o)
     for o in range(left_last - STRIDE + 1, left_last + 1):
@@ -476,7 +482,7 @@
             dma((per,)), dma((per,)),
         ],
         compiler_params=pltpu.CompilerParams(
-            collective_id=0, has_side_effects=True, vmem_limit_bytes=40 << 20
+            collective_id=0, has_side_effects=True, vmem_limit_bytes=62 << 20
         ),
     )(
         hidden_acts.reshape(total_slots * 2, units),

time: 123 us -> 120 us (0.976)
  the two profiles are of different devices: /device:TPU:24 before, /device:TPU:10 now
where the time goes in v3:
time: 120 us
  Pallas kernels  116 us (97%)
  local copies, waits for them, and re-layouts  2.12 us (2%)
    pallas_call x1, Pallas kernels, shards(): pl.pallas_call(body, out_shape=(jax.ShapeDtypeStruct((planes, 32, 128), B...  116 us

profile of v3, /device:TPU:10, one launch (start us, length us, event | category | flops | bytes accessed | tf_op | source)
XLA Modules:
  0.0 119.8 jit_solution(16814895654608765538)
XLA Ops:
  0.0 0.0 copy-start
  0.0 116.4 %shard_map.64 = (bf16[32,32,128]{2,1,0:T(8,128)(2,1)}, f32[4,8,256]{2,1,0:T(8,128)}) custom-call(bf16[128,128]{1,0:T(8,128)(2,1)} %bitcast.29, s32[8,8]{1,0:T(8,128)} %bitcast.28, f32[8,8]{1,0:T(8,128)} %bitcast.30, f32[1,56]{1,0:T(1,128)} %bitcast.31, bf16[128,7168]{1,0:T(8,128)(2,1)} %bitcast.24, bf16[32,2,64,112]{3,2,1,0:T(8,128)(2,1)} %bitcast.25), custom_call_target="tpu_custom_call" | custom-call | tf_op jit(solution)/shard_map/pallas_call | solution.py:447
  116.4 0.8 reshape.79
  117.2 0.1 reshape.80
  117.4 1.0 copy.12
  118.4 0.0 copy-done
  118.4 0.1 eq.56
  118.5 0.2 convert_reduce_fusion.1
  118.7 0.1 eq.60
  118.8 0.1 iota_compare_fusion
  118.9 0.1 convert_reduce_fusion
  119.0 0.8 fusion.1
  (4 shorter events, 0.0 us)
Async XLA Ops:
  0.0 118.4 %copy-start = (s32[2,4,8]{2,1,0:T(4,128)S(1)}, s32[2,4,8]{2,1,0:T(4,128)}, u32[]{:S(2)}) copy-start(s32[2,4,8]{2,1,0:T(4,128)} %param.10) | copy-start | bytes 772
